TPU v7x, 32 devices: a whole 2x2x4 slice. The times are simulated.
32 devices in a mesh: head: 4 (over y, x), seq: 8 (over z, core).
Axes of the slice: x: 2, y: 2, z: 4, core: 2. Of those that a mesh axis runs over, the one named last changes fastest.
Arguments:
- queries: bfloat16 [8, 512, 4096], P('seq', 'head'), may hold values from -13 to 13
- keys: bfloat16 [8, 512, 1024], P('seq', 'head'), may hold values from -8 to 8
- values: bfloat16 [8, 512, 1024], P('seq', 'head'), may hold values from -6 to 6
- output_gradient: bfloat16 [8, 512, 4096], P('seq', 'head'), may hold values from -6 to 6
- windows: int32 [32], replicated, may hold values from 1 to 4, as said below
- sinks: int32 [32], replicated, may hold values from 0 to 2, as said below
Outputs:
- grad_queries: bfloat16 [8, 512, 4096], P('seq', 'head')
- key_gradient: bfloat16 [8, 512, 1024], P('seq', 'head')
- value_gradient: bfloat16 [8, 512, 1024], P('seq', 'head')
Inputs may be any that keep to these rules, and one draw needn't show every extreme that they name: `windows`: some head has a window of exactly 4 blocks. `sinks`: some head has exactly 2 sink blocks.
All inputs are finite; a program needn't handle non-finite values.
Results may differ from a plain program's by a relative error of at most 0.009.
Values may be sent and summed in bfloat16 or wider, within the bound.
A program may use at most 64 MiB of HBM per device.

v0:
```python
import functools
import math

import jax
import jax.numpy as jnp
from jax import lax
from jax.experimental import pallas as pl
from jax.experimental.pallas import tpu as pltpu
from jax.sharding import PartitionSpec as P

QUERY_HEADS = 32
KEY_VALUE_HEADS = 8
HEAD_DIMENSION = 128
BLOCK_TOKENS = 128
WMAX = 4
SMAX = 2

NEG_FILL = -1e30
GROUP = QUERY_HEADS // KEY_VALUE_HEADS
BACK = WMAX - 1
LOOK = 2
MESH = pl.DeviceIdType.MESH


def spare_links(head_count):
    return [
        (h, c)
        for c in range(SMAX)
        for h in range(head_count)
        if h != c and not 1 <= h - c <= BACK
    ]


def kernel(
    head_count,
    seq_count,
    q_ref, k_ref, v_ref, go_ref, win_ref, sink_ref,
    dq_ref, dk_ref, dv_ref,
    own, window, sunk, gsend, grecv, rsend, rrecv, gown, rpart, yrecv,
    w_send, w_recv, s_send, s_recv, x_send, x_recv,
    g_send, g_recv, r_send, r_recv, y_send, y_recv,
):
    G = KEY_VALUE_HEADS
    D = HEAD_DIMENSION
    T = BLOCK_TOKENS
    head = lax.axis_index("head")
    seq = lax.axis_index("seq")
    total = head_count * seq_count
    b = seq * head_count + head
    even = lax.rem(seq, 2) == 0
    first = seq == 0
    scale = 1.0 / math.sqrt(D)
    spare = spare_links(head_count)

    def device(block):
        return {"head": lax.rem(block + total, total) % head_count,
                "seq": lax.div(lax.rem(block + total, total), head_count)}

    def in_seq(s):
        return {"head": head, "seq": lax.rem(s + 2 * seq_count, seq_count)}

    def in_first(h):
        return {"head": h, "seq": 0}

    def remote(src, dst, ssem, rsem, where):
        return pltpu.make_async_remote_copy(
            src_ref=src, dst_ref=dst, send_sem=ssem, recv_sem=rsem,
            device_id=where, device_id_type=MESH)

    partners = []
    for d in range(1, BACK + 1):
        partners.append((b + d < total, device(b + d)))
        partners.append((b >= d, device(b - d)))
    to_core = even & (seq + 1 < seq_count)
    to_next = even & (seq + 2 < seq_count)
    from_prev = even & (seq >= 2)
    partners.append((to_core, in_seq(seq + 1)))
    partners.append((to_next, in_seq(seq + 2)))
    partners.append((~even, in_seq(seq - 1)))
    partners.append((from_prev, in_seq(seq - 2)))
    for h, c in spare:
        partners.append((first & (head == h), in_first(c)))
        partners.append((first & (head == c), in_first(h)))

    barrier = pltpu.get_barrier_semaphore()
    expected = jnp.int32(0)
    for holds, where in partners:
        @pl.when(holds)
        def _(where=where):
            pl.semaphore_signal(barrier, inc=1, device_id=where, device_id_type=MESH)
        expected = expected + holds.astype(jnp.int32)

    for g in range(G):
        own[g, 0] = k_ref[:, g * D:(g + 1) * D]
        own[g, 1] = v_ref[:, g * D:(g + 1) * D]
    for d in range(1, BACK + 1):
        @pl.when(b < d)
        def _(d=d):
            for g in range(G):
                window[g, d - 1] = jnp.zeros((2, T, D), jnp.bfloat16)

    pl.semaphore_wait(barrier, expected)

    def w_copy(g, d):
        return remote(own.at[g], window.at[g, d - 1], w_send.at[g, d - 1], w_recv.at[g, d - 1], device(b + d))

    def s_copy(g, step):
        return remote(sunk.at[g], sunk.at[g], s_send.at[g, step - 1], s_recv.at[g], in_seq(seq + step))

    def x_copy(g, h, c):
        return remote(own.at[g], sunk.at[g, c], x_send.at[g, h], x_recv.at[g, c], in_first(h))

    def g_copy(g, d):
        return remote(gsend.at[g, d - 1], grecv.at[g, d - 1], g_send.at[g, d - 1], g_recv.at[g, d - 1], device(b - d))

    def r_copy(g, step):
        return remote(rsend.at[g], rrecv.at[g, step - 1], r_send.at[g], r_recv.at[g, step - 1], in_seq(seq - step))

    def y_copy(g, h, c):
        return remote(rsend.at[g, c], yrecv.at[h, g], y_send.at[g, c], y_recv.at[h, g], in_first(c))

    def start_sends(g, carry):
        for d in range(1, BACK + 1):
            @pl.when(b + d < total)
            def _(d=d):
                w_copy(g, d).start()
        for h, c in spare:
            @pl.when(first & (head == c))
            def _(h=h, c=c):
                x_copy(g, h, c).start()
        return carry

    lax.fori_loop(0, G, start_sends, 0)

    def wait_window(g):
        for d in range(1, BACK + 1):
            @pl.when(b >= d)
            def _(d=d):
                w_copy(g, d).wait_recv()

    def arrive(g):
        @pl.when(first)
        def _():
            wait_window(g)
            for c in range(SMAX):
                @pl.when(head == c)
                def _(c=c):
                    sunk[g, c] = own[g]
                for d in range(1, BACK + 1):
                    @pl.when(head == c + d)
                    def _(c=c, d=d):
                        sunk[g, c] = window[g, d - 1]
            for h, c in spare:
                @pl.when(head == h)
                def _(h=h, c=c):
                    x_copy(g, h, c).wait_recv()

        @pl.when(seq > 0)
        def _():
            s_copy(g, 1).wait_recv()

        @pl.when(to_next)
        def _():
            s_copy(g, 2).start()

        @pl.when(to_core)
        def _():
            s_copy(g, 1).start()

    key_row = lax.broadcasted_iota(jnp.int32, (T, GROUP * T), 0)
    query_col = lax.rem(lax.broadcasted_iota(jnp.int32, (T, GROUP * T), 1), T)

    def compute(g):
        @pl.when(seq > 0)
        def _():
            wait_window(g)

        def stacked(kind):
            return jnp.concatenate(
                [own[g, kind]] + [window[g, d, kind] for d in range(BACK)]
                + [sunk[g, c, kind] for c in range(SMAX)], 0)

        def columns(r):
            return pl.ds(pl.multiple_of((g * GROUP + r) * D, D), D)

        k_all = stacked(0)
        v_all = stacked(1)
        q_all = jnp.concatenate([q_ref[:, columns(r)] for r in range(GROUP)], 0)
        go_all = jnp.concatenate([go_ref[:, columns(r)] for r in range(GROUP)], 0)
        wide = jnp.concatenate([jnp.full((1, T), win_ref[g * GROUP + r], jnp.int32) for r in range(GROUP)], 1)
        depth = jnp.concatenate([jnp.full((1, T), sink_ref[g * GROUP + r], jnp.int32) for r in range(GROUP)], 1)
        contract = (((1,), (1,)), ((), ()))
        raw = lax.dot_general(k_all, q_all, contract, preferred_element_type=jnp.float32)
        grad_w = lax.dot_general(v_all, go_all, contract, preferred_element_type=jnp.float32)
        raw = raw * (scale * math.log2(math.e))
        slots = [jnp.where(key_row <= query_col, raw[:T], NEG_FILL)]
        for d in range(1, WMAX):
            ok = (wide > d) & (b >= d)
            slots.append(raw[d * T:(d + 1) * T] + jnp.where(ok, 0.0, NEG_FILL))
        for c in range(SMAX):
            ok = (depth > c) & (wide <= b - c)
            slots.append(raw[(WMAX + c) * T:(WMAX + c + 1) * T] + jnp.where(ok, 0.0, NEG_FILL))
        scores = jnp.concatenate(slots, 0)
        top = jnp.max(scores, 0, keepdims=True)
        e = jnp.exp2(scores - top)
        inv = 1.0 / jnp.sum(e, 0, keepdims=True)
        weights = e * inv
        row_dot = jnp.sum(weights * grad_w, 0, keepdims=True)
        weights_b = weights.astype(jnp.bfloat16)
        dscore_b = (weights * (grad_w - row_dot)).astype(jnp.bfloat16)
        dq_t = lax.dot_general(k_all, dscore_b, (((0,), (0,)), ((), ())), preferred_element_type=jnp.float32)
        dq_t = dq_t * scale
        for r in range(GROUP):
            dq_ref[:, columns(r)] = dq_t[:, r * T:(r + 1) * T].T.astype(jnp.bfloat16)
        natural = (((1,), (0,)), ((), ()))
        dk = lax.dot_general(dscore_b, q_all, natural, preferred_element_type=jnp.float32) * scale
        dv = lax.dot_general(weights_b, go_all, natural, preferred_element_type=jnp.float32)
        for c in range(SMAX):
            rows = slice((WMAX + c) * T, (WMAX + c + 1) * T)
            rpart[g, c, 0] = dk[rows]
            rpart[g, c, 1] = dv[rows]

        @pl.when(~even)
        def _():
            rsend[g] = rpart[g].astype(jnp.bfloat16)
            r_copy(g, 1).start()

        for d in range(1, WMAX):
            rows = slice(d * T, (d + 1) * T)
            gsend[g, d - 1, 0] = dk[rows].astype(jnp.bfloat16)
            gsend[g, d - 1, 1] = dv[rows].astype(jnp.bfloat16)
            later = first & (head >= d) & (head < d + SMAX)

            @pl.when((b >= d) & ~later)
            def _(d=d):
                g_copy(g, d).start()
        gown[g, 0] = dk[:T]
        gown[g, 1] = dv[:T]

    def reduce(g):
        @pl.when(to_core)
        def _():
            r_copy(g, 1).wait_recv()
            rpart[g] = rpart[g] + rrecv[g, 0].astype(jnp.float32)

        @pl.when(to_next)
        def _():
            r_copy(g, 2).wait_recv()
            rpart[g] = rpart[g] + rrecv[g, 1].astype(jnp.float32)

        @pl.when(from_prev)
        def _():
            rsend[g] = rpart[g].astype(jnp.bfloat16)
            r_copy(g, 2).start()

        @pl.when(first)
        def _():
            for c in range(SMAX):
                @pl.when(head == c)
                def _(c=c):
                    gown[g] = gown[g] + rpart[g, c]
                for d in range(1, BACK + 1):
                    @pl.when(head == c + d)
                    def _(c=c, d=d):
                        gsend[g, d - 1] = (gsend[g, d - 1].astype(jnp.float32) + rpart[g, c]).astype(jnp.bfloat16)
                        g_copy(g, d).start()
            for h, c in spare:
                @pl.when(head == h)
                def _(h=h, c=c):
                    rsend[g, c] = rpart[g, c].astype(jnp.bfloat16)
                    y_copy(g, h, c).start()

    lag = jnp.minimum(1 + 2 * lax.div(seq_count - 1 - seq, 2), G)

    def prologue(g, carry):
        arrive(g)
        return carry

    lax.fori_loop(0, LOOK, prologue, 0)

    def step(i, carry):
        @pl.when(i + LOOK < G)
        def _():
            arrive(i + LOOK)

        @pl.when(i < G)
        def _():
            compute(i)

        j = i - lag

        @pl.when(even & (j >= 0) & (j < G))
        def _():
            reduce(j)
        return carry

    lax.fori_loop(0, 2 * G, step, 0)

    def finish(g, carry):
        for d in range(1, BACK + 1):
            @pl.when(b + d < total)
            def _(d=d):
                g_copy(g, d).wait_recv()
                gown[g] = gown[g] + grecv[g, d - 1].astype(jnp.float32)
        for h, c in spare:
            @pl.when(first & (head == c))
            def _(h=h, c=c):
                y_copy(g, h, c).wait_recv()
                gown[g] = gown[g] + yrecv[h, g].astype(jnp.float32)
        cols = pl.ds(pl.multiple_of(g * D, D), D)
        dk_ref[:, cols] = gown[g, 0].astype(jnp.bfloat16)
        dv_ref[:, cols] = gown[g, 1].astype(jnp.bfloat16)
        return carry

    lax.fori_loop(0, G, finish, 0)

    def drain(g, carry):
        for d in range(1, BACK + 1):
            @pl.when(b + d < total)
            def _(d=d):
                w_copy(g, d).wait_send()

            @pl.when(b >= d)
            def _(d=d):
                g_copy(g, d).wait_send()

        @pl.when(to_next)
        def _():
            s_copy(g, 2).wait_send()

        @pl.when(to_core)
        def _():
            s_copy(g, 1).wait_send()

        @pl.when(~even)
        def _():
            r_copy(g, 1).wait_send()

        @pl.when(from_prev)
        def _():
            r_copy(g, 2).wait_send()

        for h, c in spare:
            @pl.when(first & (head == c))
            def _(h=h, c=c):
                x_copy(g, h, c).wait_send()

            @pl.when(first & (head == h))
            def _(h=h, c=c):
                y_copy(g, h, c).wait_send()
        return carry

    lax.fori_loop(0, G, drain, 0)


def shards(head_count, seq_count, queries, keys, values, output_gradient, windows, sinks):
    G, D, T = KEY_VALUE_HEADS, HEAD_DIMENSION, BLOCK_TOKENS
    assert queries.shape[1] == T
    bf16, f32 = jnp.bfloat16, jnp.float32
    dma = pltpu.SemaphoreType.DMA
    vmem = pl.BlockSpec(memory_space=pltpu.VMEM)
    smem = pl.BlockSpec(memory_space=pltpu.SMEM)
    dq, dk, dv = pl.pallas_call(
        functools.partial(kernel, head_count, seq_count),
        out_shape=(
            jax.ShapeDtypeStruct((T, QUERY_HEADS * D), bf16),
            jax.ShapeDtypeStruct((T, G * D), bf16),
            jax.ShapeDtypeStruct((T, G * D), bf16),
        ),
        in_specs=[vmem] * 4 + [smem] * 2,
        out_specs=(vmem,) * 3,
        scratch_shapes=[
            pltpu.VMEM((G, 2, T, D), bf16),
            pltpu.VMEM((G, BACK, 2, T, D), bf16),
            pltpu.VMEM((G, SMAX, 2, T, D), bf16),
            pltpu.VMEM((G, BACK, 2, T, D), bf16),
            pltpu.VMEM((G, BACK, 2, T, D), bf16),
            pltpu.VMEM((G, SMAX, 2, T, D), bf16),
            pltpu.VMEM((G, 2, SMAX, 2, T, D), bf16),
            pltpu.VMEM((G, 2, T, D), f32),
            pltpu.VMEM((G, SMAX, 2, T, D), f32),
            pltpu.VMEM((head_count, G, 2, T, D), bf16),
            dma((G, BACK)), dma((G, BACK)),
            dma((G, 2)), dma((G,)),
            dma((G, head_count)), dma((G, SMAX)),
            dma((G, BACK)), dma((G, BACK)),
            dma((G,)), dma((G, 2)),
            dma((G, SMAX)), dma((head_count, G)),
        ],
        compiler_params=pltpu.CompilerParams(
            collective_id=0, has_side_effects=True, vmem_limit_bytes=52 * 2**20),
    )(queries[0], keys[0], values[0], output_gradient[0], windows, sinks)
    return dq[None], dk[None], dv[None]


def solution(mesh):
    return jax.shard_map(
        functools.partial(shards, mesh.shape["head"], mesh.shape["seq"]),
        mesh=mesh,
        in_specs=(
            P("seq", "head", None),
            P("seq", "head", None),
            P("seq", "head", None),
            P("seq", "head", None),
            P(),
            P(),
        ),
        out_specs=(P("seq", "head", None), P("seq", "head", None), P("seq", "head", None)),
        check_vma=False,
    )
```

profile of v0, /device:TPU:0, one launch (start us, length us, event | category | flops | bytes accessed | tf_op | source)
XLA Modules:
  0.0 91.7 jit_solution(5096212533632192899)
XLA Ops:
  0.6 0.0 copy-start.2
  0.6 0.0 copy-start.3
  0.7 0.6 copy-done.2
  1.3 0.0 copy-done.3
  1.3 0.0 copy-start
  1.3 0.9 %copy-done = bf16[1,128,1024]{2,1,0:T(8,128)(2,1)S(1)} copy-done((bf16[1,128,1024]{2,1,0:T(8,128)(2,1)S(1)}, bf16[1,128,1024]{2,1,0:T(8,128)(2,1)}, u32[]{:S(2)}) %copy-start) | copy-done | bytes 262168
  2.3 0.0 copy-start.1
  2.3 0.9 %copy-done.1 = bf16[1,128,1024]{2,1,0:T(8,128)(2,1)S(1)} copy-done((bf16[1,128,1024]{2,1,0:T(8,128)(2,1)S(1)}, bf16[1,128,1024]{2,1,0:T(8,128)(2,1)}, u32[]{:S(2)}) %copy-start.1) | copy-done | bytes 262168
  3.2 84.8 %shard_map.85 = (bf16[128,4096]{1,0:T(8,128)(2,1)}, bf16[128,1024]{1,0:T(8,128)(2,1)S(1)}, bf16[128,1024]{1,0:T(8,128)(2,1)S(1)}) custom-call(bf16[128,4096]{1,0:T(8,128)(2,1)} %bitcast.11, bf16[128,1024]{1,0:T(8,128)(2,1)S(1)} %bitcast.7, bf16[128,1024]{1,0:T(8,128)(2,1)S(1)} %bitcast.8, bf16[128,4096]{1,0:T(8,128)(2,1)} %bitcast.12, s32[32]{0:T(128)S(1)} %copy-done.2, ...), custom_call_target="tpu_custom_call" | custom-call | tf_op jit(solution)/shard_map/pallas_call | solution.py:363
  88.0 2.3 %copy.12 = bf16[1,128,4096]{2,1,0:T(8,128)(2,1)} copy(bf16[1,128,4096]{2,1,0:T(8,128)(2,1)} %bitcast.13) | data formatting | bytes 2097152
  90.3 0.7 copy.13
  91.0 0.7 copy.14
Async XLA Ops:
  0.6 0.7 copy-start.2
  0.6 0.7 copy-start.3
  1.3 0.9 %copy-start = (bf16[1,128,1024]{2,1,0:T(8,128)(2,1)S(1)}, bf16[1,128,1024]{2,1,0:T(8,128)(2,1)}, u32[]{:S(2)}) copy-start(bf16[1,128,1024]{2,1,0:T(8,128)(2,1)} %param.7) | copy-start | bytes 786436
  2.3 0.9 %copy-start.1 = (bf16[1,128,1024]{2,1,0:T(8,128)(2,1)S(1)}, bf16[1,128,1024]{2,1,0:T(8,128)(2,1)}, u32[]{:S(2)}) copy-start(bf16[1,128,1024]{2,1,0:T(8,128)(2,1)} %param.8) | copy-start | bytes 786436
where the time goes:
time: 92 us; the launch traced here: 91.7 us
  Pallas kernels  84.8 us (92%)
  local copies, waits for them, and re-layouts  6.25 us (7%)
    pallas_call x1, Pallas kernels, shards(): pl.pallas_call(functools.partial(kernel, head_count, seq_count), out_shap...  84.8 us
    unnamed x11, local copies, waits for them, and re-layouts  6.25 us

commit v1 on v0

--- a/solution.py
+++ b/solution.py
@@ -19,6 +19,8 @@
 GROUP = QUERY_HEADS // KEY_VALUE_HEADS
 BACK = WMAX - 1
 LOOK = 2
+HOLD = 2
+PAIRS = ((1, 3, 0, 0), (2, 3, 0, 1), (2, 1, 1, 0), (3, 1, 1, 1))
 MESH = pl.DeviceIdType.MESH
 
 
@@ -34,11 +36,12 @@
 def kernel(
     head_count,
     seq_count,
-    q_ref, k_ref, v_ref, go_ref, win_ref, sink_ref,
+    q_hbm, k_hbm, v_hbm, go_hbm, win_ref, sink_ref,
     dq_ref, dk_ref, dv_ref,
-    own, window, sunk, gsend, grecv, rsend, rrecv, gown, rpart, yrecv,
+    q_ref, go_ref, prel, own, window, sunk, gsend, grecv, rsend, rrecv, gown, rpart, yrecv,
     w_send, w_recv, s_send, s_recv, x_send, x_recv,
     g_send, g_recv, r_send, r_recv, y_send, y_recv,
+    f_send, p_send, p_recv, in_sem,
 ):
     G = KEY_VALUE_HEADS
     D = HEAD_DIMENSION
@@ -82,6 +85,43 @@
         partners.append((first & (head == h), in_first(c)))
         partners.append((first & (head == c), in_first(h)))
 
+    def in_copies(g):
+        cols = pl.ds(pl.multiple_of(g * D, D), D)
+        wide_cols = pl.ds(pl.multiple_of(g * GROUP * D, GROUP * D), GROUP * D)
+        return (
+            pltpu.make_async_copy(k_hbm.at[:, cols], own.at[g, 0], in_sem.at[g, 0]),
+            pltpu.make_async_copy(v_hbm.at[:, cols], own.at[g, 1], in_sem.at[g, 1]),
+            pltpu.make_async_copy(q_hbm.at[:, wide_cols], q_ref.at[:, wide_cols], in_sem.at[g, 2]),
+            pltpu.make_async_copy(go_hbm.at[:, wide_cols], go_ref.at[:, wide_cols], in_sem.at[g, 3]),
+        )
+
+    def relayed(block, g, pair):
+        near, far, parity, turn = pair
+        if head_count != 4:
+            return jnp.bool_(False)
+        return ((block >= 0) & (lax.rem(block + total, 2) == parity) & (lax.rem(g, 2) == turn)
+                & (block + max(near, far) < total))
+
+    def relayed_to(block, g, d):
+        hit = jnp.bool_(False)
+        for pair in PAIRS:
+            if pair[1] == d:
+                hit = hit | relayed(block, g, pair)
+        return hit
+
+    def load_kv(g, carry):
+        for copy in in_copies(g)[:2]:
+            copy.start()
+        return carry
+
+    def load_q(g, carry):
+        for copy in in_copies(g)[2:]:
+            copy.start()
+        return carry
+
+    lax.fori_loop(0, G, load_kv, 0)
+    lax.fori_loop(0, G, load_q, 0)
+
     barrier = pltpu.get_barrier_semaphore()
     expected = jnp.int32(0)
     for holds, where in partners:
@@ -90,9 +130,6 @@
             pl.semaphore_signal(barrier, inc=1, device_id=where, device_id_type=MESH)
         expected = expected + holds.astype(jnp.int32)
 
-    for g in range(G):
-        own[g, 0] = k_ref[:, g * D:(g + 1) * D]
-        own[g, 1] = v_ref[:, g * D:(g + 1) * D]
     for d in range(1, BACK + 1):
         @pl.when(b < d)
         def _(d=d):
@@ -119,9 +156,19 @@
     def y_copy(g, h, c):
         return remote(rsend.at[g, c], yrecv.at[h, g], y_send.at[g, c], y_recv.at[h, g], in_first(c))
 
+    def f_copy(g, near, far):
+        return remote(window.at[g, near - 1], window.at[g, far - 1], f_send.at[g], w_recv.at[g, far - 1],
+                      device(b + far - near))
+
+    def p_copy(g, near, far):
+        return remote(gsend.at[g, far - 1], prel.at[g, near - 1], p_send.at[g], p_recv.at[g, near - 1],
+                      device(b - far + near))
+
     def start_sends(g, carry):
+        for copy in in_copies(g)[:2]:
+            copy.wait()
         for d in range(1, BACK + 1):
-            @pl.when(b + d < total)
+            @pl.when((b + d < total) & ~relayed_to(b, g, d))
             def _(d=d):
                 w_copy(g, d).start()
         for h, c in spare:
@@ -132,13 +179,26 @@
 
     lax.fori_loop(0, G, start_sends, 0)
 
+    def passes(g, d):
+        hit = jnp.bool_(False)
+        for pair in PAIRS:
+            if pair[0] == d:
+                hit = hit | relayed(b - d, g, pair)
+        return hit
+
     def wait_window(g):
         for d in range(1, BACK + 1):
-            @pl.when(b >= d)
+            @pl.when((b >= d) & ~passes(g, d))
             def _(d=d):
                 w_copy(g, d).wait_recv()
 
     def arrive(g):
+        for pair in PAIRS:
+            @pl.when(relayed(b - pair[0], g, pair))
+            def _(near=pair[0], far=pair[1]):
+                w_copy(g, near).wait_recv()
+                f_copy(g, near, far).start()
+
         @pl.when(first)
         def _():
             wait_window(g)
@@ -174,6 +234,9 @@
         @pl.when(seq > 0)
         def _():
             wait_window(g)
+
+        for copy in in_copies(g)[2:]:
+            copy.wait()
 
         def stacked(kind):
             return jnp.concatenate(
@@ -230,10 +293,18 @@
             gsend[g, d - 1, 0] = dk[rows].astype(jnp.bfloat16)
             gsend[g, d - 1, 1] = dv[rows].astype(jnp.bfloat16)
             later = first & (head >= d) & (head < d + SMAX)
-
-            @pl.when((b >= d) & ~later)
+            direct = (b >= d) & ~later
+            kept = b - d >= SMAX
+
+            @pl.when(direct & ~(kept & (relayed_to(b - d, g, d) | passes(g, d))))
             def _(d=d):
                 g_copy(g, d).start()
+
+            for pair in PAIRS:
+                if pair[1] == d:
+                    @pl.when(kept & relayed(b - d, g, pair))
+                    def _(near=pair[0], far=pair[1]):
+                        p_copy(g, near, far).start()
         gown[g, 0] = dk[:T]
         gown[g, 1] = dv[:T]
 
@@ -270,6 +341,16 @@
                     rsend[g, c] = rpart[g, c].astype(jnp.bfloat16)
                     y_copy(g, h, c).start()
 
+    def merge(g):
+        for d in range(1, BACK + 1):
+            @pl.when((b - d >= SMAX) & passes(g, d))
+            def _(d=d):
+                p_copy(g, d, d).wait_recv()
+                gsend[g, d - 1] = (
+                    gsend[g, d - 1].astype(jnp.float32) + prel[g, d - 1].astype(jnp.float32)
+                ).astype(jnp.bfloat16)
+                g_copy(g, d).start()
+
     lag = jnp.minimum(1 + 2 * lax.div(seq_count - 1 - seq, 2), G)
 
     def prologue(g, carry):
@@ -287,6 +368,10 @@
         def _():
             compute(i)
 
+        @pl.when((i >= HOLD) & (i - HOLD < G))
+        def _():
+            merge(i - HOLD)
+
         j = i - lag
 
         @pl.when(even & (j >= 0) & (j < G))
@@ -298,7 +383,7 @@
 
     def finish(g, carry):
         for d in range(1, BACK + 1):
-            @pl.when(b + d < total)
+            @pl.when((b + d < total) & ~((b >= SMAX) & relayed_to(b, g, d)))
             def _(d=d):
                 g_copy(g, d).wait_recv()
                 gown[g] = gown[g] + grecv[g, d - 1].astype(jnp.float32)
@@ -316,13 +401,22 @@
 
     def drain(g, carry):
         for d in range(1, BACK + 1):
-            @pl.when(b + d < total)
+            @pl.when((b + d < total) & ~relayed_to(b, g, d))
             def _(d=d):
                 w_copy(g, d).wait_send()
 
-            @pl.when(b >= d)
+            @pl.when((b >= d) & ~((b - d >= SMAX) & relayed_to(b - d, g, d)))
             def _(d=d):
                 g_copy(g, d).wait_send()
+
+        for pair in PAIRS:
+            @pl.when(relayed(b - pair[0], g, pair))
+            def _(near=pair[0], far=pair[1]):
+                f_copy(g, near, far).wait_send()
+
+            @pl.when((b - pair[1] >= SMAX) & relayed(b - pair[1], g, pair))
+            def _(near=pair[0], far=pair[1]):
+                p_copy(g, near, far).wait_send()
 
         @pl.when(to_next)
         def _():
@@ -367,9 +461,12 @@
             jax.ShapeDtypeStruct((T, G * D), bf16),
             jax.ShapeDtypeStruct((T, G * D), bf16),
         ),
-        in_specs=[vmem] * 4 + [smem] * 2,
+        in_specs=[pl.BlockSpec(memory_space=pltpu.HBM)] * 4 + [smem] * 2,
         out_specs=(vmem,) * 3,
         scratch_shapes=[
+            pltpu.VMEM((T, QUERY_HEADS * D), bf16),
+            pltpu.VMEM((T, QUERY_HEADS * D), bf16),
+            pltpu.VMEM((G, BACK, 2, T, D), bf16),
             pltpu.VMEM((G, 2, T, D), bf16),
             pltpu.VMEM((G, BACK, 2, T, D), bf16),
             pltpu.VMEM((G, SMAX, 2, T, D), bf16),
@@ -386,9 +483,10 @@
             dma((G, BACK)), dma((G, BACK)),
             dma((G,)), dma((G, 2)),
             dma((G, SMAX)), dma((head_count, G)),
+            dma((G,)), dma((G,)), dma((G, BACK)), dma((G, 4)),
         ],
         compiler_params=pltpu.CompilerParams(
-            collective_id=0, has_side_effects=True, vmem_limit_bytes=52 * 2**20),
+            collective_id=0, has_side_effects=True, vmem_limit_bytes=40 * 2**20),
     )(queries[0], keys[0], values[0], output_gradient[0], windows, sinks)
     return dq[None], dk[None], dv[None]
 

time: 92 us -> 101 us (1.098)
  Pallas kernels: 84.8 us -> 92.3 us
  local copies, waits for them, and re-layouts: 6.25 us -> 7.38 us
    pallas_call x1, Pallas kernels: 84.8 us -> 92.3 us  [shards(): pl.pallas_call(functools.partial(kernel, head_count, seq_count), out_shap...]
    unnamed x11 -> x15, local copies, waits for them, and re-layouts: 6.25 us -> 7.38 us
where the time goes in v1:
time: 101 us; the launch traced here: 100 us
  Pallas kernels  92.3 us (91%)
  local copies, waits for them, and re-layouts  7.38 us (7%)
    pallas_call x1, Pallas kernels, shards(): pl.pallas_call(functools.partial(kernel, head_count, seq_count), out_shap...  92.3 us
    unnamed x15, local copies, waits for them, and re-layouts  7.38 us

profile of v1, /device:TPU:0, one launch (start us, length us, event | category | flops | bytes accessed | tf_op | source)
XLA Modules:
  0.0 100.3 jit_solution(3504557778150607480)
XLA Ops:
  0.6 0.0 copy-start.4
  0.6 0.0 copy-start.5
  0.7 0.6 copy-done.4
  1.3 0.0 copy-done.5
  1.3 0.0 copy-start
  1.3 1.2 %copy-done = bf16[1,128,4096]{2,1,0:T(8,128)(2,1)S(1)} copy-done((bf16[1,128,4096]{2,1,0:T(8,128)(2,1)S(1)}, bf16[1,128,4096]{2,1,0:T(8,128)(2,1)}, u32[]{:S(2)}) %copy-start) | copy-done | bytes 1048600
  2.5 0.0 copy-start.1
  2.5 1.2 %copy-done.1 = bf16[1,128,4096]{2,1,0:T(8,128)(2,1)S(1)} copy-done((bf16[1,128,4096]{2,1,0:T(8,128)(2,1)S(1)}, bf16[1,128,4096]{2,1,0:T(8,128)(2,1)}, u32[]{:S(2)}) %copy-start.1) | copy-done | bytes 1048600
  3.8 0.0 copy-start.2
  3.8 0.9 copy-done.2
  4.7 0.0 copy-start.3
  4.7 0.9 copy-done.3
  5.7 92.3 %shard_map.85 = (bf16[128,4096]{1,0:T(8,128)(2,1)S(1)}, bf16[128,1024]{1,0:T(8,128)(2,1)S(1)}, bf16[128,1024]{1,0:T(8,128)(2,1)S(1)}) custom-call(bf16[128,4096]{1,0:T(8,128)(2,1)S(1)} %bitcast.7, bf16[128,1024]{1,0:T(8,128)(2,1)S(1)} %bitcast.10, bf16[128,1024]{1,0:T(8,128)(2,1)S(1)} %bitcast.11, bf16[128,4096]{1,0:T(8,128)(2,1)S(1)} %bitcast.8, ...), custom_call_target="tpu_custom_call" | custom-call | tf_op jit(solution)/shard_map/pallas_call | solution.py:457
  97.9 1.0 copy.12
  98.9 0.7 copy.13
  99.6 0.7 copy.14
Async XLA Ops:
  0.6 0.7 copy-start.4
  0.6 0.7 copy-start.5
  1.3 1.2 %copy-start = (bf16[1,128,4096]{2,1,0:T(8,128)(2,1)S(1)}, bf16[1,128,4096]{2,1,0:T(8,128)(2,1)}, u32[]{:S(2)}) copy-start(bf16[1,128,4096]{2,1,0:T(8,128)(2,1)} %param.6) | copy-start | bytes 3145732
  2.5 1.2 %copy-start.1 = (bf16[1,128,4096]{2,1,0:T(8,128)(2,1)S(1)}, bf16[1,128,4096]{2,1,0:T(8,128)(2,1)}, u32[]{:S(2)}) copy-start(bf16[1,128,4096]{2,1,0:T(8,128)(2,1)} %param.9) | copy-start | bytes 3145732
  3.8 0.9 copy-start.2
  4.7 0.9 copy-start.3

commit v2 on v0

--- a/solution.py
+++ b/solution.py
@@ -19,6 +19,7 @@
 GROUP = QUERY_HEADS // KEY_VALUE_HEADS
 BACK = WMAX - 1
 LOOK = 2
+AHEAD = 4
 MESH = pl.DeviceIdType.MESH
 
 
@@ -34,11 +35,11 @@
 def kernel(
     head_count,
     seq_count,
-    q_ref, k_ref, v_ref, go_ref, win_ref, sink_ref,
+    q_hbm, k_hbm, v_hbm, go_hbm, win_ref, sink_ref,
     dq_ref, dk_ref, dv_ref,
-    own, window, sunk, gsend, grecv, rsend, rrecv, gown, rpart, yrecv,
+    q_ref, go_ref, sc, gw, wb, ds, own, window, sunk, gsend, grecv, rsend, rrecv, gown, rpart, yrecv,
     w_send, w_recv, s_send, s_recv, x_send, x_recv,
-    g_send, g_recv, r_send, r_recv, y_send, y_recv,
+    g_send, g_recv, r_send, r_recv, y_send, y_recv, in_sem,
 ):
     G = KEY_VALUE_HEADS
     D = HEAD_DIMENSION
@@ -82,6 +83,29 @@
         partners.append((first & (head == h), in_first(c)))
         partners.append((first & (head == c), in_first(h)))
 
+    def kv_copies(g):
+        cols = pl.ds(pl.multiple_of(g * D, D), D)
+        return (pltpu.make_async_copy(k_hbm.at[:, cols], own.at[g, 0], in_sem.at[g, 0]),
+                pltpu.make_async_copy(v_hbm.at[:, cols], own.at[g, 1], in_sem.at[g, 1]))
+
+    def q_copies(g):
+        cols = pl.ds(pl.multiple_of(g * GROUP * D, GROUP * D), GROUP * D)
+        return (pltpu.make_async_copy(q_hbm.at[:, cols], q_ref.at[:, cols], in_sem.at[g, 2]),
+                pltpu.make_async_copy(go_hbm.at[:, cols], go_ref.at[:, cols], in_sem.at[g, 3]))
+
+    def load_kv(g, carry):
+        for copy in kv_copies(g):
+            copy.start()
+        return carry
+
+    def load_q(g, carry):
+        for copy in q_copies(g):
+            copy.start()
+        return carry
+
+    lax.fori_loop(0, G, load_kv, 0)
+    lax.fori_loop(0, G, load_q, 0)
+
     barrier = pltpu.get_barrier_semaphore()
     expected = jnp.int32(0)
     for holds, where in partners:
@@ -90,9 +114,6 @@
             pl.semaphore_signal(barrier, inc=1, device_id=where, device_id_type=MESH)
         expected = expected + holds.astype(jnp.int32)
 
-    for g in range(G):
-        own[g, 0] = k_ref[:, g * D:(g + 1) * D]
-        own[g, 1] = v_ref[:, g * D:(g + 1) * D]
     for d in range(1, BACK + 1):
         @pl.when(b < d)
         def _(d=d):
@@ -120,6 +141,8 @@
         return remote(rsend.at[g, c], yrecv.at[h, g], y_send.at[g, c], y_recv.at[h, g], in_first(c))
 
     def start_sends(g, carry):
+        for copy in kv_copies(g):
+            copy.wait()
         for d in range(1, BACK + 1):
             @pl.when(b + d < total)
             def _(d=d):
@@ -130,7 +153,7 @@
                 x_copy(g, h, c).start()
         return carry
 
-    lax.fori_loop(0, G, start_sends, 0)
+    lax.fori_loop(0, AHEAD, start_sends, 0)
 
     def wait_window(g):
         for d in range(1, BACK + 1):
@@ -167,13 +190,15 @@
         def _():
             s_copy(g, 1).start()
 
-    key_row = lax.broadcasted_iota(jnp.int32, (T, GROUP * T), 0)
-    query_col = lax.rem(lax.broadcasted_iota(jnp.int32, (T, GROUP * T), 1), T)
+    causal = lax.broadcasted_iota(jnp.int32, (T, T), 0) <= lax.broadcasted_iota(jnp.int32, (T, T), 1)
 
     def compute(g):
         @pl.when(seq > 0)
         def _():
             wait_window(g)
+
+        for copy in q_copies(g):
+            copy.wait()
 
         def stacked(kind):
             return jnp.concatenate(
@@ -190,25 +215,52 @@
         wide = jnp.concatenate([jnp.full((1, T), win_ref[g * GROUP + r], jnp.int32) for r in range(GROUP)], 1)
         depth = jnp.concatenate([jnp.full((1, T), sink_ref[g * GROUP + r], jnp.int32) for r in range(GROUP)], 1)
         contract = (((1,), (1,)), ((), ()))
-        raw = lax.dot_general(k_all, q_all, contract, preferred_element_type=jnp.float32)
-        grad_w = lax.dot_general(v_all, go_all, contract, preferred_element_type=jnp.float32)
-        raw = raw * (scale * math.log2(math.e))
-        slots = [jnp.where(key_row <= query_col, raw[:T], NEG_FILL)]
-        for d in range(1, WMAX):
-            ok = (wide > d) & (b >= d)
-            slots.append(raw[d * T:(d + 1) * T] + jnp.where(ok, 0.0, NEG_FILL))
-        for c in range(SMAX):
-            ok = (depth > c) & (wide <= b - c)
-            slots.append(raw[(WMAX + c) * T:(WMAX + c + 1) * T] + jnp.where(ok, 0.0, NEG_FILL))
-        scores = jnp.concatenate(slots, 0)
-        top = jnp.max(scores, 0, keepdims=True)
-        e = jnp.exp2(scores - top)
-        inv = 1.0 / jnp.sum(e, 0, keepdims=True)
-        weights = e * inv
-        row_dot = jnp.sum(weights * grad_w, 0, keepdims=True)
-        weights_b = weights.astype(jnp.bfloat16)
-        dscore_b = (weights * (grad_w - row_dot)).astype(jnp.bfloat16)
-        dq_t = lax.dot_general(k_all, dscore_b, (((0,), (0,)), ((), ())), preferred_element_type=jnp.float32)
+        for part in range(2):
+            lanes = slice(part * 2 * T, (part + 1) * 2 * T)
+            sc[:, lanes] = lax.dot_general(
+                k_all, q_all[lanes], contract, preferred_element_type=jnp.float32)
+            gw[:, lanes] = lax.dot_general(
+                v_all, go_all[lanes], contract, preferred_element_type=jnp.float32)
+        slots = WMAX + SMAX
+        k_turned = k_all.astype(jnp.float32).T.astype(jnp.bfloat16)
+        for r in range(GROUP):
+            lanes = slice(r * T, (r + 1) * T)
+            bias = [None]
+            for d in range(1, WMAX):
+                bias.append(jnp.where((wide[:, lanes] > d) & (b >= d), 0.0, NEG_FILL))
+            for c in range(SMAX):
+                bias.append(jnp.where((depth[:, lanes] > c) & (wide[:, lanes] <= b - c), 0.0, NEG_FILL))
+            top = None
+            for n in range(slots):
+                rows = slice(n * T, (n + 1) * T)
+                tile = sc[rows, lanes] * (scale * math.log2(math.e))
+                if n == 0:
+                    tile = jnp.where(causal, tile, NEG_FILL)
+                else:
+                    tile = tile + bias[n]
+                sc[rows, lanes] = tile
+                high = jnp.max(tile.reshape(T // 8, 8, T), 0)
+                top = high if top is None else jnp.maximum(top, high)
+            top = jnp.max(top, 0, keepdims=True)
+            mass = dot = None
+            for n in range(slots):
+                rows = slice(n * T, (n + 1) * T)
+                e = jnp.exp2(sc[rows, lanes] - top)
+                sc[rows, lanes] = e
+                mass_n = jnp.sum(e.reshape(T // 8, 8, T), 0)
+                dot_n = jnp.sum((e * gw[rows, lanes]).reshape(T // 8, 8, T), 0)
+                mass = mass_n if mass is None else mass + mass_n
+                dot = dot_n if dot is None else dot + dot_n
+            inv = 1.0 / jnp.sum(mass, 0, keepdims=True)
+            row_dot = jnp.sum(dot, 0, keepdims=True) * inv
+            for n in range(slots):
+                rows = slice(n * T, (n + 1) * T)
+                weights = sc[rows, lanes] * inv
+                wb[rows, lanes] = weights.astype(jnp.bfloat16)
+                ds[rows, lanes] = (weights * (gw[rows, lanes] - row_dot)).astype(jnp.bfloat16)
+        weights_b = wb[...]
+        dscore_b = ds[...]
+        dq_t = lax.dot_general(k_turned, dscore_b, (((1,), (0,)), ((), ())), preferred_element_type=jnp.float32)
         dq_t = dq_t * scale
         for r in range(GROUP):
             dq_ref[:, columns(r)] = dq_t[:, r * T:(r + 1) * T].T.astype(jnp.bfloat16)
@@ -279,6 +331,10 @@
     lax.fori_loop(0, LOOK, prologue, 0)
 
     def step(i, carry):
+        @pl.when(i + AHEAD < G)
+        def _():
+            start_sends(i + AHEAD, 0)
+
         @pl.when(i + LOOK < G)
         def _():
             arrive(i + LOOK)
@@ -367,9 +423,15 @@
             jax.ShapeDtypeStruct((T, G * D), bf16),
             jax.ShapeDtypeStruct((T, G * D), bf16),
         ),
-        in_specs=[vmem] * 4 + [smem] * 2,
+        in_specs=[pl.BlockSpec(memory_space=pltpu.HBM)] * 4 + [smem] * 2,
         out_specs=(vmem,) * 3,
         scratch_shapes=[
+            pltpu.VMEM((T, QUERY_HEADS * D), bf16),
+            pltpu.VMEM((T, QUERY_HEADS * D), bf16),
+            pltpu.VMEM(((WMAX + SMAX) * T, GROUP * T), f32),
+            pltpu.VMEM(((WMAX + SMAX) * T, GROUP * T), f32),
+            pltpu.VMEM(((WMAX + SMAX) * T, GROUP * T), bf16),
+            pltpu.VMEM(((WMAX + SMAX) * T, GROUP * T), bf16),
             pltpu.VMEM((G, 2, T, D), bf16),
             pltpu.VMEM((G, BACK, 2, T, D), bf16),
             pltpu.VMEM((G, SMAX, 2, T, D), bf16),
@@ -385,10 +447,10 @@
             dma((G, head_count)), dma((G, SMAX)),
             dma((G, BACK)), dma((G, BACK)),
             dma((G,)), dma((G, 2)),
-            dma((G, SMAX)), dma((head_count, G)),
+            dma((G, SMAX)), dma((head_count, G)), dma((G, 4)),
         ],
         compiler_params=pltpu.CompilerParams(
-            collective_id=0, has_side_effects=True, vmem_limit_bytes=52 * 2**20),
+            collective_id=0, has_side_effects=True, vmem_limit_bytes=58 * 2**20),
     )(queries[0], keys[0], values[0], output_gradient[0], windows, sinks)
     return dq[None], dk[None], dv[None]
 

time: 92 us -> 85.4 us (0.928)
  Pallas kernels: 84.8 us -> 80.5 us
  local copies, waits for them, and re-layouts: 6.25 us -> 4.08 us
    pallas_call x1, Pallas kernels: 84.8 us -> 80.5 us  [shards(): pl.pallas_call(functools.partial(kernel, head_count, seq_count), out_shap...]
    unnamed x11 -> x7, local copies, waits for them, and re-layouts: 6.25 us -> 4.08 us
where the time goes in v2:
time: 85.4 us; the launch traced here: 85.2 us
  Pallas kernels  80.5 us (94%)
  local copies, waits for them, and re-layouts  4.08 us (5%)
    pallas_call x1, Pallas kernels, shards(): pl.pallas_call(functools.partial(kernel, head_count, seq_count), out_shap...  80.5 us
    unnamed x7, local copies, waits for them, and re-layouts  4.08 us

profile of v2, /device:TPU:0, one launch (start us, length us, event | category | flops | bytes accessed | tf_op | source)
XLA Modules:
  0.0 85.2 jit_solution(8564153025831355396)
XLA Ops:
  0.6 80.5 %shard_map.85 = (bf16[128,4096]{1,0:T(8,128)(2,1)}, bf16[128,1024]{1,0:T(8,128)(2,1)}, bf16[128,1024]{1,0:T(8,128)(2,1)}) custom-call(bf16[128,4096]{1,0:T(8,128)(2,1)} %bitcast.7, bf16[128,1024]{1,0:T(8,128)(2,1)} %bitcast.10, bf16[128,1024]{1,0:T(8,128)(2,1)} %bitcast.11, bf16[128,4096]{1,0:T(8,128)(2,1)} %bitcast.8, s32[32]{0:T(128)} %win_ref.1, s32[32]{0:T(128)} %sink_ref.1), custom_call_target="tpu_custom_call" | custom-call | tf_op jit(solution)/shard_map/pallas_call | solution.py:419
  81.1 0.0 copy-start.1
  81.1 2.3 %copy.12 = bf16[1,128,4096]{2,1,0:T(8,128)(2,1)} copy(bf16[1,128,4096]{2,1,0:T(8,128)(2,1)} %bitcast.9) | data formatting | bytes 2097152
  83.4 0.0 copy-done.1
  83.4 0.0 copy-start
  83.4 0.7 copy.13
  84.1 0.3 copy-done
  84.5 0.7 copy.14
Async XLA Ops:
  81.1 2.3 %copy-start.1 = (bf16[128,1024]{1,0:T(8,128)(2,1)S(1)}, bf16[128,1024]{1,0:T(8,128)(2,1)}, u32[]{:S(2)}) copy-start(bf16[128,1024]{1,0:T(8,128)(2,1)} %get-tuple-element.7) | copy-start | bytes 786436
  83.4 1.0 %copy-start = (bf16[128,1024]{1,0:T(8,128)(2,1)S(1)}, bf16[128,1024]{1,0:T(8,128)(2,1)}, u32[]{:S(2)}) copy-start(bf16[128,1024]{1,0:T(8,128)(2,1)} %get-tuple-element.8) | copy-start | bytes 786436

commit v3 on v2

--- a/solution.py
+++ b/solution.py
@@ -48,7 +48,11 @@
     seq = lax.axis_index("seq")
     total = head_count * seq_count
     b = seq * head_count + head
-    even = lax.rem(seq, 2) == 0
+    levels = max(1, (seq_count - 1).bit_length())
+    to_child = [(lax.rem(seq, 2 << k) == 0) & (seq + (1 << k) < seq_count) for k in range(levels)]
+    to_parent = [lax.rem(seq, 2 << k) == (1 << k) for k in range(levels)]
+    height = sum(to_child[k].astype(jnp.int32) for k in range(levels))
+    leaf = height == 0
     first = seq == 0
     scale = 1.0 / math.sqrt(D)
     spare = spare_links(head_count)
@@ -58,7 +62,7 @@
                 "seq": lax.div(lax.rem(block + total, total), head_count)}
 
     def in_seq(s):
-        return {"head": head, "seq": lax.rem(s + 2 * seq_count, seq_count)}
+        return {"head": head, "seq": lax.rem(s + seq_count, seq_count)}
 
     def in_first(h):
         return {"head": h, "seq": 0}
@@ -72,13 +76,9 @@
     for d in range(1, BACK + 1):
         partners.append((b + d < total, device(b + d)))
         partners.append((b >= d, device(b - d)))
-    to_core = even & (seq + 1 < seq_count)
-    to_next = even & (seq + 2 < seq_count)
-    from_prev = even & (seq >= 2)
-    partners.append((to_core, in_seq(seq + 1)))
-    partners.append((to_next, in_seq(seq + 2)))
-    partners.append((~even, in_seq(seq - 1)))
-    partners.append((from_prev, in_seq(seq - 2)))
+    for k in range(levels):
+        partners.append((to_child[k], in_seq(seq + (1 << k))))
+        partners.append((to_parent[k], in_seq(seq - (1 << k))))
     for h, c in spare:
         partners.append((first & (head == h), in_first(c)))
         partners.append((first & (head == c), in_first(h)))
@@ -125,8 +125,8 @@
     def w_copy(g, d):
         return remote(own.at[g], window.at[g, d - 1], w_send.at[g, d - 1], w_recv.at[g, d - 1], device(b + d))
 
-    def s_copy(g, step):
-        return remote(sunk.at[g], sunk.at[g], s_send.at[g, step - 1], s_recv.at[g], in_seq(seq + step))
+    def s_copy(g, k):
+        return remote(sunk.at[g], sunk.at[g], s_send.at[g, k], s_recv.at[g], in_seq(seq + (1 << k)))
 
     def x_copy(g, h, c):
         return remote(own.at[g], sunk.at[g, c], x_send.at[g, h], x_recv.at[g, c], in_first(h))
@@ -134,8 +134,8 @@
     def g_copy(g, d):
         return remote(gsend.at[g, d - 1], grecv.at[g, d - 1], g_send.at[g, d - 1], g_recv.at[g, d - 1], device(b - d))
 
-    def r_copy(g, step):
-        return remote(rsend.at[g], rrecv.at[g, step - 1], r_send.at[g], r_recv.at[g, step - 1], in_seq(seq - step))
+    def r_copy(g, k):
+        return remote(rsend.at[g], rrecv.at[g, k], r_send.at[g], r_recv.at[g, k], in_seq(seq - (1 << k)))
 
     def y_copy(g, h, c):
         return remote(rsend.at[g, c], yrecv.at[h, g], y_send.at[g, c], y_recv.at[h, g], in_first(c))
@@ -180,15 +180,12 @@
 
         @pl.when(seq > 0)
         def _():
-            s_copy(g, 1).wait_recv()
-
-        @pl.when(to_next)
-        def _():
-            s_copy(g, 2).start()
-
-        @pl.when(to_core)
-        def _():
-            s_copy(g, 1).start()
+            s_copy(g, 0).wait_recv()
+
+        for k in reversed(range(levels)):
+            @pl.when(to_child[k])
+            def _(k=k):
+                s_copy(g, k).start()
 
     causal = lax.broadcasted_iota(jnp.int32, (T, T), 0) <= lax.broadcasted_iota(jnp.int32, (T, T), 1)
 
@@ -223,29 +220,28 @@
                 v_all, go_all[lanes], contract, preferred_element_type=jnp.float32)
         slots = WMAX + SMAX
         k_turned = k_all.astype(jnp.float32).T.astype(jnp.bfloat16)
-        for r in range(GROUP):
+        folded = scale * math.log2(math.e)
+
+        def softmax(r):
             lanes = slice(r * T, (r + 1) * T)
-            bias = [None]
+            bias = [jnp.zeros((1, T), jnp.float32)]
             for d in range(1, WMAX):
                 bias.append(jnp.where((wide[:, lanes] > d) & (b >= d), 0.0, NEG_FILL))
             for c in range(SMAX):
                 bias.append(jnp.where((depth[:, lanes] > c) & (wide[:, lanes] <= b - c), 0.0, NEG_FILL))
+
+            def raw(n):
+                tile = sc[n * T:(n + 1) * T, lanes]
+                return jnp.where(causal, tile, NEG_FILL) if n == 0 else tile
+
             top = None
             for n in range(slots):
-                rows = slice(n * T, (n + 1) * T)
-                tile = sc[rows, lanes] * (scale * math.log2(math.e))
-                if n == 0:
-                    tile = jnp.where(causal, tile, NEG_FILL)
-                else:
-                    tile = tile + bias[n]
-                sc[rows, lanes] = tile
-                high = jnp.max(tile.reshape(T // 8, 8, T), 0)
+                high = jnp.max(raw(n), 0, keepdims=True) * folded + bias[n]
                 top = high if top is None else jnp.maximum(top, high)
-            top = jnp.max(top, 0, keepdims=True)
             mass = dot = None
             for n in range(slots):
                 rows = slice(n * T, (n + 1) * T)
-                e = jnp.exp2(sc[rows, lanes] - top)
+                e = jnp.exp2(raw(n) * folded + (bias[n] - top))
                 sc[rows, lanes] = e
                 mass_n = jnp.sum(e.reshape(T // 8, 8, T), 0)
                 dot_n = jnp.sum((e * gw[rows, lanes]).reshape(T // 8, 8, T), 0)
@@ -258,24 +254,35 @@
                 weights = sc[rows, lanes] * inv
                 wb[rows, lanes] = weights.astype(jnp.bfloat16)
                 ds[rows, lanes] = (weights * (gw[rows, lanes] - row_dot)).astype(jnp.bfloat16)
-        weights_b = wb[...]
-        dscore_b = ds[...]
-        dq_t = lax.dot_general(k_turned, dscore_b, (((1,), (0,)), ((), ())), preferred_element_type=jnp.float32)
-        dq_t = dq_t * scale
-        for r in range(GROUP):
-            dq_ref[:, columns(r)] = dq_t[:, r * T:(r + 1) * T].T.astype(jnp.bfloat16)
+
         natural = (((1,), (0,)), ((), ()))
-        dk = lax.dot_general(dscore_b, q_all, natural, preferred_element_type=jnp.float32) * scale
-        dv = lax.dot_general(weights_b, go_all, natural, preferred_element_type=jnp.float32)
+        dk = dv = None
+        for part in range(2):
+            lanes = slice(part * 2 * T, (part + 1) * 2 * T)
+            for r in range(2 * part, 2 * part + 2):
+                softmax(r)
+            dscore_b = ds[:, lanes]
+            dk_n = lax.dot_general(dscore_b, q_all[lanes], natural, preferred_element_type=jnp.float32)
+            dv_n = lax.dot_general(wb[:, lanes], go_all[lanes], natural, preferred_element_type=jnp.float32)
+            dk = dk_n if dk is None else dk + dk_n
+            dv = dv_n if dv is None else dv + dv_n
+            dq_t = lax.dot_general(k_turned, dscore_b, natural, preferred_element_type=jnp.float32) * scale
+            for r in range(2):
+                dq_ref[:, columns(2 * part + r)] = dq_t[:, r * T:(r + 1) * T].T.astype(jnp.bfloat16)
+        dk = dk * scale
         for c in range(SMAX):
             rows = slice((WMAX + c) * T, (WMAX + c + 1) * T)
             rpart[g, c, 0] = dk[rows]
             rpart[g, c, 1] = dv[rows]
 
-        @pl.when(~even)
+        @pl.when(leaf & ~first)
         def _():
             rsend[g] = rpart[g].astype(jnp.bfloat16)
-            r_copy(g, 1).start()
+
+        for k in range(levels):
+            @pl.when(leaf & to_parent[k])
+            def _(k=k):
+                r_copy(g, k).start()
 
         for d in range(1, WMAX):
             rows = slice(d * T, (d + 1) * T)
@@ -290,20 +297,17 @@
         gown[g, 1] = dv[:T]
 
     def reduce(g):
-        @pl.when(to_core)
-        def _():
-            r_copy(g, 1).wait_recv()
-            rpart[g] = rpart[g] + rrecv[g, 0].astype(jnp.float32)
-
-        @pl.when(to_next)
-        def _():
-            r_copy(g, 2).wait_recv()
-            rpart[g] = rpart[g] + rrecv[g, 1].astype(jnp.float32)
-
-        @pl.when(from_prev)
-        def _():
-            rsend[g] = rpart[g].astype(jnp.bfloat16)
-            r_copy(g, 2).start()
+        for k in range(levels):
+            @pl.when(to_child[k])
+            def _(k=k):
+                r_copy(g, k).wait_recv()
+                rpart[g] = rpart[g] + rrecv[g, k].astype(jnp.float32)
+
+        for k in range(levels):
+            @pl.when(to_parent[k])
+            def _(k=k):
+                rsend[g] = rpart[g].astype(jnp.bfloat16)
+                r_copy(g, k).start()
 
         @pl.when(first)
         def _():
@@ -322,7 +326,7 @@
                     rsend[g, c] = rpart[g, c].astype(jnp.bfloat16)
                     y_copy(g, h, c).start()
 
-    lag = jnp.minimum(1 + 2 * lax.div(seq_count - 1 - seq, 2), G)
+    lag = jnp.clip(2 * height - 1, 0, G)
 
     def prologue(g, carry):
         arrive(g)
@@ -345,7 +349,7 @@
 
         j = i - lag
 
-        @pl.when(even & (j >= 0) & (j < G))
+        @pl.when((first | ~leaf) & (j >= 0) & (j < G))
         def _():
             reduce(j)
         return carry
@@ -380,21 +384,14 @@
             def _(d=d):
                 g_copy(g, d).wait_send()
 
-        @pl.when(to_next)
-        def _():
-            s_copy(g, 2).wait_send()
-
-        @pl.when(to_core)
-        def _():
-            s_copy(g, 1).wait_send()
-
-        @pl.when(~even)
-        def _():
-            r_copy(g, 1).wait_send()
-
-        @pl.when(from_prev)
-        def _():
-            r_copy(g, 2).wait_send()
+        for k in range(levels):
+            @pl.when(to_child[k])
+            def _(k=k):
+                s_copy(g, k).wait_send()
+
+            @pl.when(to_parent[k])
+            def _(k=k):
+                r_copy(g, k).wait_send()
 
         for h, c in spare:
             @pl.when(first & (head == c))
@@ -412,6 +409,7 @@
 def shards(head_count, seq_count, queries, keys, values, output_gradient, windows, sinks):
     G, D, T = KEY_VALUE_HEADS, HEAD_DIMENSION, BLOCK_TOKENS
     assert queries.shape[1] == T
+    levels = max(1, (seq_count - 1).bit_length())
     bf16, f32 = jnp.bfloat16, jnp.float32
     dma = pltpu.SemaphoreType.DMA
     vmem = pl.BlockSpec(memory_space=pltpu.VMEM)
@@ -438,15 +436,15 @@
             pltpu.VMEM((G, BACK, 2, T, D), bf16),
             pltpu.VMEM((G, BACK, 2, T, D), bf16),
             pltpu.VMEM((G, SMAX, 2, T, D), bf16),
-            pltpu.VMEM((G, 2, SMAX, 2, T, D), bf16),
+            pltpu.VMEM((G, levels, SMAX, 2, T, D), bf16),
             pltpu.VMEM((G, 2, T, D), f32),
             pltpu.VMEM((G, SMAX, 2, T, D), f32),
             pltpu.VMEM((head_count, G, 2, T, D), bf16),
             dma((G, BACK)), dma((G, BACK)),
-            dma((G, 2)), dma((G,)),
+            dma((G, levels)), dma((G,)),
             dma((G, head_count)), dma((G, SMAX)),
             dma((G, BACK)), dma((G, BACK)),
-            dma((G,)), dma((G, 2)),
+            dma((G,)), dma((G, levels)),
             dma((G, SMAX)), dma((head_count, G)), dma((G, 4)),
         ],
         compiler_params=pltpu.CompilerParams(

time: 85.4 us -> 81.9 us (0.959)
  Pallas kernels: 80.5 us -> 77 us
    pallas_call x1, Pallas kernels: 80.5 us -> 77 us  [shards(): pl.pallas_call(functools.partial(kernel, head_count, seq_count), out_shap...]
where the time goes in v3:
time: 81.9 us; the launch traced here: 81.7 us
  Pallas kernels  77 us (94%)
  local copies, waits for them, and re-layouts  4.08 us (5%)
    pallas_call x1, Pallas kernels, shards(): pl.pallas_call(functools.partial(kernel, head_count, seq_count), out_shap...  77 us
    unnamed x7, local copies, waits for them, and re-layouts  4.08 us

profile of v3, /device:TPU:0, one launch (start us, length us, event | category | flops | bytes accessed | tf_op | source)
XLA Modules:
  0.0 81.7 jit_solution(15935096734417855353)
XLA Ops:
  0.6 77.0 %shard_map.85 = (bf16[128,4096]{1,0:T(8,128)(2,1)}, bf16[128,1024]{1,0:T(8,128)(2,1)}, bf16[128,1024]{1,0:T(8,128)(2,1)}) custom-call(bf16[128,4096]{1,0:T(8,128)(2,1)} %bitcast.7, bf16[128,1024]{1,0:T(8,128)(2,1)} %bitcast.10, bf16[128,1024]{1,0:T(8,128)(2,1)} %bitcast.11, bf16[128,4096]{1,0:T(8,128)(2,1)} %bitcast.8, s32[32]{0:T(128)} %win_ref.1, s32[32]{0:T(128)} %sink_ref.1), custom_call_target="tpu_custom_call" | custom-call | tf_op jit(solution)/shard_map/pallas_call | solution.py:417
  77.6 0.0 copy-start.1
  77.6 2.3 %copy.12 = bf16[1,128,4096]{2,1,0:T(8,128)(2,1)} copy(bf16[1,128,4096]{2,1,0:T(8,128)(2,1)} %bitcast.9) | data formatting | bytes 2097152
  79.9 0.0 copy-done.1
  79.9 0.0 copy-start
  79.9 0.7 copy.13
  80.6 0.3 copy-done
  81.0 0.7 copy.14
Async XLA Ops:
  77.6 2.3 %copy-start.1 = (bf16[128,1024]{1,0:T(8,128)(2,1)S(1)}, bf16[128,1024]{1,0:T(8,128)(2,1)}, u32[]{:S(2)}) copy-start(bf16[128,1024]{1,0:T(8,128)(2,1)} %get-tuple-element.7) | copy-start | bytes 786436
  79.9 1.0 %copy-start = (bf16[128,1024]{1,0:T(8,128)(2,1)S(1)}, bf16[128,1024]{1,0:T(8,128)(2,1)}, u32[]{:S(2)}) copy-start(bf16[128,1024]{1,0:T(8,128)(2,1)} %get-tuple-element.8) | copy-start | bytes 786436

commit v4 on v3

--- a/solution.py
+++ b/solution.py
@@ -20,6 +20,8 @@
 BACK = WMAX - 1
 LOOK = 2
 AHEAD = 4
+HOLD = 2
+PAIRS = ((1, 3, 0, 0), (2, 3, 0, 1), (2, 1, 1, 0), (3, 1, 1, 1))
 MESH = pl.DeviceIdType.MESH
 
 
@@ -37,9 +39,10 @@
     seq_count,
     q_hbm, k_hbm, v_hbm, go_hbm, win_ref, sink_ref,
     dq_ref, dk_ref, dv_ref,
-    q_ref, go_ref, sc, gw, wb, ds, own, window, sunk, gsend, grecv, rsend, rrecv, gown, rpart, yrecv,
+    q_ref, go_ref, prel, sc, gw, wb, ds, own, window, sunk, gsend, grecv, rsend, rrecv, gown, rpart, yrecv,
     w_send, w_recv, s_send, s_recv, x_send, x_recv,
     g_send, g_recv, r_send, r_recv, y_send, y_recv, in_sem,
+    f_send, p_send, p_recv,
 ):
     G = KEY_VALUE_HEADS
     D = HEAD_DIMENSION
@@ -140,11 +143,40 @@
     def y_copy(g, h, c):
         return remote(rsend.at[g, c], yrecv.at[h, g], y_send.at[g, c], y_recv.at[h, g], in_first(c))
 
+    def relayed(block, g, pair):
+        near, far, parity, turn = pair
+        if head_count != 4:
+            return jnp.bool_(False)
+        return ((block >= SMAX) & (lax.rem(block + total, 2) == parity) & (lax.rem(g, 2) == turn)
+                & (block + max(near, far) < total))
+
+    def relayed_to(block, g, d):
+        hit = jnp.bool_(False)
+        for pair in PAIRS:
+            if pair[1] == d:
+                hit = hit | relayed(block, g, pair)
+        return hit
+
+    def passes(g, d):
+        hit = jnp.bool_(False)
+        for pair in PAIRS:
+            if pair[0] == d:
+                hit = hit | relayed(b - d, g, pair)
+        return hit
+
+    def f_copy(g, near, far):
+        return remote(window.at[g, near - 1], window.at[g, far - 1], f_send.at[g, near - 1], w_recv.at[g, far - 1],
+                      device(b + far - near))
+
+    def p_copy(g, near, far):
+        return remote(gsend.at[g, far - 1], prel.at[g, near - 1], p_send.at[g, far - 1], p_recv.at[g, near - 1],
+                      device(b - far + near))
+
     def start_sends(g, carry):
         for copy in kv_copies(g):
             copy.wait()
         for d in range(1, BACK + 1):
-            @pl.when(b + d < total)
+            @pl.when((b + d < total) & ~relayed_to(b, g, d))
             def _(d=d):
                 w_copy(g, d).start()
         for h, c in spare:
@@ -157,11 +189,17 @@
 
     def wait_window(g):
         for d in range(1, BACK + 1):
-            @pl.when(b >= d)
+            @pl.when((b >= d) & ~passes(g, d))
             def _(d=d):
                 w_copy(g, d).wait_recv()
 
     def arrive(g):
+        for pair in PAIRS:
+            @pl.when(relayed(b - pair[0], g, pair))
+            def _(near=pair[0], far=pair[1]):
+                w_copy(g, near).wait_recv()
+                f_copy(g, near, far).start()
+
         @pl.when(first)
         def _():
             wait_window(g)
@@ -290,9 +328,15 @@
             gsend[g, d - 1, 1] = dv[rows].astype(jnp.bfloat16)
             later = first & (head >= d) & (head < d + SMAX)
 
-            @pl.when((b >= d) & ~later)
+            @pl.when((b >= d) & ~later & ~relayed_to(b - d, g, d) & ~passes(g, d))
             def _(d=d):
                 g_copy(g, d).start()
+
+            for pair in PAIRS:
+                if pair[1] == d:
+                    @pl.when(relayed(b - d, g, pair))
+                    def _(near=pair[0], far=pair[1]):
+                        p_copy(g, near, far).start()
         gown[g, 0] = dk[:T]
         gown[g, 1] = dv[:T]
 
@@ -326,6 +370,16 @@
                     rsend[g, c] = rpart[g, c].astype(jnp.bfloat16)
                     y_copy(g, h, c).start()
 
+    def merge(g):
+        for d in range(1, BACK + 1):
+            @pl.when(passes(g, d))
+            def _(d=d):
+                p_copy(g, d, d).wait_recv()
+                gsend[g, d - 1] = (
+                    gsend[g, d - 1].astype(jnp.float32) + prel[g, d - 1].astype(jnp.float32)
+                ).astype(jnp.bfloat16)
+                g_copy(g, d).start()
+
     lag = jnp.clip(2 * height - 1, 0, G)
 
     def prologue(g, carry):
@@ -335,14 +389,14 @@
     lax.fori_loop(0, LOOK, prologue, 0)
 
     def step(i, carry):
+        @pl.when(i + LOOK < G)
+        def _():
+            arrive(i + LOOK)
+
         @pl.when(i + AHEAD < G)
         def _():
             start_sends(i + AHEAD, 0)
 
-        @pl.when(i + LOOK < G)
-        def _():
-            arrive(i + LOOK)
-
         @pl.when(i < G)
         def _():
             compute(i)
@@ -352,13 +406,17 @@
         @pl.when((first | ~leaf) & (j >= 0) & (j < G))
         def _():
             reduce(j)
+
+        @pl.when((i >= HOLD) & (i - HOLD < G))
+        def _():
+            merge(i - HOLD)
         return carry
 
     lax.fori_loop(0, 2 * G, step, 0)
 
     def finish(g, carry):
         for d in range(1, BACK + 1):
-            @pl.when(b + d < total)
+            @pl.when((b + d < total) & ~relayed_to(b, g, d))
             def _(d=d):
                 g_copy(g, d).wait_recv()
                 gown[g] = gown[g] + grecv[g, d - 1].astype(jnp.float32)
@@ -376,13 +434,22 @@
 
     def drain(g, carry):
         for d in range(1, BACK + 1):
-            @pl.when(b + d < total)
+            @pl.when((b + d < total) & ~relayed_to(b, g, d))
             def _(d=d):
                 w_copy(g, d).wait_send()
 
-            @pl.when(b >= d)
+            @pl.when((b >= d) & ~relayed_to(b - d, g, d))
             def _(d=d):
                 g_copy(g, d).wait_send()
+
+        for pair in PAIRS:
+            @pl.when(relayed(b - pair[0], g, pair))
+            def _(near=pair[0], far=pair[1]):
+                f_copy(g, near, far).wait_send()
+
+            @pl.when(relayed(b - pair[1], g, pair))
+            def _(near=pair[0], far=pair[1]):
+                p_copy(g, near, far).wait_send()
 
         for k in range(levels):
             @pl.when(to_child[k])
@@ -426,6 +493,7 @@
         scratch_shapes=[
             pltpu.VMEM((T, QUERY_HEADS * D), bf16),
             pltpu.VMEM((T, QUERY_HEADS * D), bf16),
+            pltpu.VMEM((G, BACK, 2, T, D), bf16),
             pltpu.VMEM(((WMAX + SMAX) * T, GROUP * T), f32),
             pltpu.VMEM(((WMAX + SMAX) * T, GROUP * T), f32),
             pltpu.VMEM(((WMAX + SMAX) * T, GROUP * T), bf16),
@@ -446,6 +514,7 @@
             dma((G, BACK)), dma((G, BACK)),
             dma((G,)), dma((G, levels)),
             dma((G, SMAX)), dma((head_count, G)), dma((G, 4)),
+            dma((G, BACK)), dma((G, BACK)), dma((G, BACK)),
         ],
         compiler_params=pltpu.CompilerParams(
             collective_id=0, has_side_effects=True, vmem_limit_bytes=58 * 2**20),

time: 81.9 us -> 80.2 us (0.979)
  Pallas kernels: 77 us -> 75.3 us
    pallas_call x1, Pallas kernels: 77 us -> 75.3 us  [shards(): pl.pallas_call(functools.partial(kernel, head_count, seq_count), out_shap...]
where the time goes in v4:
time: 80.2 us; the launch traced here: 80.1 us
  Pallas kernels  75.3 us (94%)
  local copies, waits for them, and re-layouts  4.08 us (5%)
    pallas_call x1, Pallas kernels, shards(): pl.pallas_call(functools.partial(kernel, head_count, seq_count), out_shap...  75.3 us
    unnamed x7, local copies, waits for them, and re-layouts  4.08 us

profile of v4, /device:TPU:0, one launch (start us, length us, event | category | flops | bytes accessed | tf_op | source)
XLA Modules:
  0.0 80.1 jit_solution(5382085570042617472)
XLA Ops:
  0.6 75.3 %shard_map.85 = (bf16[128,4096]{1,0:T(8,128)(2,1)}, bf16[128,1024]{1,0:T(8,128)(2,1)}, bf16[128,1024]{1,0:T(8,128)(2,1)}) custom-call(bf16[128,4096]{1,0:T(8,128)(2,1)} %bitcast.7, bf16[128,1024]{1,0:T(8,128)(2,1)} %bitcast.10, bf16[128,1024]{1,0:T(8,128)(2,1)} %bitcast.11, bf16[128,4096]{1,0:T(8,128)(2,1)} %bitcast.8, s32[32]{0:T(128)} %win_ref.1, s32[32]{0:T(128)} %sink_ref.1), custom_call_target="tpu_custom_call" | custom-call | tf_op jit(solution)/shard_map/pallas_call | solution.py:484
  76.0 0.0 copy-start.1
  76.0 2.3 %copy.12 = bf16[1,128,4096]{2,1,0:T(8,128)(2,1)} copy(bf16[1,128,4096]{2,1,0:T(8,128)(2,1)} %bitcast.9) | data formatting | bytes 2097152
  78.3 0.0 copy-done.1
  78.3 0.0 copy-start
  78.3 0.7 copy.13
  79.0 0.3 copy-done
  79.4 0.7 copy.14
Async XLA Ops:
  76.0 2.3 %copy-start.1 = (bf16[128,1024]{1,0:T(8,128)(2,1)S(1)}, bf16[128,1024]{1,0:T(8,128)(2,1)}, u32[]{:S(2)}) copy-start(bf16[128,1024]{1,0:T(8,128)(2,1)} %get-tuple-element.7) | copy-start | bytes 786436
  78.3 1.0 %copy-start = (bf16[128,1024]{1,0:T(8,128)(2,1)S(1)}, bf16[128,1024]{1,0:T(8,128)(2,1)}, u32[]{:S(2)}) copy-start(bf16[128,1024]{1,0:T(8,128)(2,1)} %get-tuple-element.8) | copy-start | bytes 786436

commit v5 on v4

--- a/solution.py
+++ b/solution.py
@@ -18,9 +18,9 @@
 NEG_FILL = -1e30
 GROUP = QUERY_HEADS // KEY_VALUE_HEADS
 BACK = WMAX - 1
-LOOK = 2
-AHEAD = 4
-HOLD = 2
+LOOK = 1
+AHEAD = 3
+HOLD = 3
 PAIRS = ((1, 3, 0, 0), (2, 3, 0, 1), (2, 1, 1, 0), (3, 1, 1, 1))
 MESH = pl.DeviceIdType.MESH
 
@@ -185,7 +185,7 @@
                 x_copy(g, h, c).start()
         return carry
 
-    lax.fori_loop(0, AHEAD, start_sends, 0)
+    lax.fori_loop(0, AHEAD - 1, start_sends, 0)
 
     def wait_window(g):
         for d in range(1, BACK + 1):
@@ -380,13 +380,14 @@
                 ).astype(jnp.bfloat16)
                 g_copy(g, d).start()
 
-    lag = jnp.clip(2 * height - 1, 0, G)
+    lag = jnp.clip(2 * height, 0, G)
 
     def prologue(g, carry):
         arrive(g)
         return carry
 
     lax.fori_loop(0, LOOK, prologue, 0)
+    start_sends(AHEAD - 1, 0)
 
     def step(i, carry):
         @pl.when(i + LOOK < G)

time: 80.2 us -> 82.6 us (1.030)
  Pallas kernels: 75.3 us -> 77.7 us
    pallas_call x1, Pallas kernels: 75.3 us -> 77.7 us  [shards(): pl.pallas_call(functools.partial(kernel, head_count, seq_count), out_shap...]
where the time goes in v5:
time: 82.6 us; the launch traced here: 82.4 us
  Pallas kernels  77.7 us (94%)
  local copies, waits for them, and re-layouts  4.08 us (5%)
    pallas_call x1, Pallas kernels, shards(): pl.pallas_call(functools.partial(kernel, head_count, seq_count), out_shap...  77.7 us
    unnamed x7, local copies, waits for them, and re-layouts  4.08 us

profile of v5, /device:TPU:0, one launch (start us, length us, event | category | flops | bytes accessed | tf_op | source)
XLA Modules:
  0.0 82.4 jit_solution(13315354694723988367)
XLA Ops:
  0.6 77.7 %shard_map.85 = (bf16[128,4096]{1,0:T(8,128)(2,1)}, bf16[128,1024]{1,0:T(8,128)(2,1)}, bf16[128,1024]{1,0:T(8,128)(2,1)}) custom-call(bf16[128,4096]{1,0:T(8,128)(2,1)} %bitcast.7, bf16[128,1024]{1,0:T(8,128)(2,1)} %bitcast.10, bf16[128,1024]{1,0:T(8,128)(2,1)} %bitcast.11, bf16[128,4096]{1,0:T(8,128)(2,1)} %bitcast.8, s32[32]{0:T(128)} %win_ref.1, s32[32]{0:T(128)} %sink_ref.1), custom_call_target="tpu_custom_call" | custom-call | tf_op jit(solution)/shard_map/pallas_call | solution.py:485
  78.3 0.0 copy-start.1
  78.3 2.3 %copy.12 = bf16[1,128,4096]{2,1,0:T(8,128)(2,1)} copy(bf16[1,128,4096]{2,1,0:T(8,128)(2,1)} %bitcast.9) | data formatting | bytes 2097152
  80.7 0.0 copy-done.1
  80.7 0.0 copy-start
  80.7 0.7 copy.13
  81.4 0.3 copy-done
  81.7 0.7 copy.14
Async XLA Ops:
  78.3 2.3 %copy-start.1 = (bf16[128,1024]{1,0:T(8,128)(2,1)S(1)}, bf16[128,1024]{1,0:T(8,128)(2,1)}, u32[]{:S(2)}) copy-start(bf16[128,1024]{1,0:T(8,128)(2,1)} %get-tuple-element.7) | copy-start | bytes 786436
  80.7 1.0 %copy-start = (bf16[128,1024]{1,0:T(8,128)(2,1)S(1)}, bf16[128,1024]{1,0:T(8,128)(2,1)}, u32[]{:S(2)}) copy-start(bf16[128,1024]{1,0:T(8,128)(2,1)} %get-tuple-element.8) | copy-start | bytes 786436

commit v6 on v4

--- a/solution.py
+++ b/solution.py
@@ -18,8 +18,8 @@
 NEG_FILL = -1e30
 GROUP = QUERY_HEADS // KEY_VALUE_HEADS
 BACK = WMAX - 1
-LOOK = 2
-AHEAD = 4
+LOOK = 3
+AHEAD = 6
 HOLD = 2
 PAIRS = ((1, 3, 0, 0), (2, 3, 0, 1), (2, 1, 1, 0), (3, 1, 1, 1))
 MESH = pl.DeviceIdType.MESH

time: 80.2 us -> 82.1 us (1.024)
  Pallas kernels: 75.3 us -> 77.2 us
    pallas_call x1, Pallas kernels: 75.3 us -> 77.2 us  [shards(): pl.pallas_call(functools.partial(kernel, head_count, seq_count), out_shap...]
where the time goes in v6:
time: 82.1 us; the launch traced here: 81.9 us
  Pallas kernels  77.2 us (94%)
  local copies, waits for them, and re-layouts  4.08 us (5%)
    pallas_call x1, Pallas kernels, shards(): pl.pallas_call(functools.partial(kernel, head_count, seq_count), out_shap...  77.2 us
    unnamed x7, local copies, waits for them, and re-layouts  4.08 us

profile of v6, /device:TPU:0, one launch (start us, length us, event | category | flops | bytes accessed | tf_op | source)
XLA Modules:
  0.0 81.9 jit_solution(10113937211216469831)
XLA Ops:
  0.6 77.2 %shard_map.85 = (bf16[128,4096]{1,0:T(8,128)(2,1)}, bf16[128,1024]{1,0:T(8,128)(2,1)}, bf16[128,1024]{1,0:T(8,128)(2,1)}) custom-call(bf16[128,4096]{1,0:T(8,128)(2,1)} %bitcast.7, bf16[128,1024]{1,0:T(8,128)(2,1)} %bitcast.10, bf16[128,1024]{1,0:T(8,128)(2,1)} %bitcast.11, bf16[128,4096]{1,0:T(8,128)(2,1)} %bitcast.8, s32[32]{0:T(128)} %win_ref.1, s32[32]{0:T(128)} %sink_ref.1), custom_call_target="tpu_custom_call" | custom-call | tf_op jit(solution)/shard_map/pallas_call | solution.py:484
  77.8 0.0 copy-start.1
  77.8 2.3 %copy.12 = bf16[1,128,4096]{2,1,0:T(8,128)(2,1)} copy(bf16[1,128,4096]{2,1,0:T(8,128)(2,1)} %bitcast.9) | data formatting | bytes 2097152
  80.2 0.0 copy-done.1
  80.2 0.0 copy-start
  80.2 0.7 copy.13
  80.9 0.3 copy-done
  81.2 0.7 copy.14
Async XLA Ops:
  77.8 2.3 %copy-start.1 = (bf16[128,1024]{1,0:T(8,128)(2,1)S(1)}, bf16[128,1024]{1,0:T(8,128)(2,1)}, u32[]{:S(2)}) copy-start(bf16[128,1024]{1,0:T(8,128)(2,1)} %get-tuple-element.7) | copy-start | bytes 786436
  80.2 1.0 %copy-start = (bf16[128,1024]{1,0:T(8,128)(2,1)S(1)}, bf16[128,1024]{1,0:T(8,128)(2,1)}, u32[]{:S(2)}) copy-start(bf16[128,1024]{1,0:T(8,128)(2,1)} %get-tuple-element.8) | copy-start | bytes 786436

commit v7 on v4

--- a/solution.py
+++ b/solution.py
@@ -380,7 +380,7 @@
                 ).astype(jnp.bfloat16)
                 g_copy(g, d).start()
 
-    lag = jnp.clip(2 * height - 1, 0, G)
+    lag = jnp.clip(2 * height, 0, G)
 
     def prologue(g, carry):
         arrive(g)
@@ -397,15 +397,15 @@
         def _():
             start_sends(i + AHEAD, 0)
 
+        j = i - lag
+
+        @pl.when((first | ~leaf) & (j >= 0) & (j < G))
+        def _():
+            reduce(j)
+
         @pl.when(i < G)
         def _():
             compute(i)
-
-        j = i - lag
-
-        @pl.when((first | ~leaf) & (j >= 0) & (j < G))
-        def _():
-            reduce(j)
 
         @pl.when((i >= HOLD) & (i - HOLD < G))
         def _():

time: 80.2 us -> 80.9 us (level)
  no operation moved by 1% of the time
where the time goes in v7:
time: 80.9 us; the launch traced here: 80.7 us
  Pallas kernels  76 us (94%)
  local copies, waits for them, and re-layouts  4.08 us (5%)
    pallas_call x1, Pallas kernels, shards(): pl.pallas_call(functools.partial(kernel, head_count, seq_count), out_shap...  76 us
    unnamed x7, local copies, waits for them, and re-layouts  4.08 us

profile of v7, /device:TPU:0, one launch (start us, length us, event | category | flops | bytes accessed | tf_op | source)
XLA Modules:
  0.0 80.7 jit_solution(15113433478860143255)
XLA Ops:
  0.6 76.0 %shard_map.85 = (bf16[128,4096]{1,0:T(8,128)(2,1)}, bf16[128,1024]{1,0:T(8,128)(2,1)}, bf16[128,1024]{1,0:T(8,128)(2,1)}) custom-call(bf16[128,4096]{1,0:T(8,128)(2,1)} %bitcast.7, bf16[128,1024]{1,0:T(8,128)(2,1)} %bitcast.10, bf16[128,1024]{1,0:T(8,128)(2,1)} %bitcast.11, bf16[128,4096]{1,0:T(8,128)(2,1)} %bitcast.8, s32[32]{0:T(128)} %win_ref.1, s32[32]{0:T(128)} %sink_ref.1), custom_call_target="tpu_custom_call" | custom-call | tf_op jit(solution)/shard_map/pallas_call | solution.py:484
  76.6 0.0 copy-start.1
  76.7 2.3 %copy.12 = bf16[1,128,4096]{2,1,0:T(8,128)(2,1)} copy(bf16[1,128,4096]{2,1,0:T(8,128)(2,1)} %bitcast.9) | data formatting | bytes 2097152
  79.0 0.0 copy-done.1
  79.0 0.0 copy-start
  79.0 0.7 copy.13
  79.7 0.3 copy-done
  80.0 0.7 copy.14
Async XLA Ops:
  76.6 2.3 %copy-start.1 = (bf16[128,1024]{1,0:T(8,128)(2,1)S(1)}, bf16[128,1024]{1,0:T(8,128)(2,1)}, u32[]{:S(2)}) copy-start(bf16[128,1024]{1,0:T(8,128)(2,1)} %get-tuple-element.7) | copy-start | bytes 786436
  79.0 1.0 %copy-start = (bf16[128,1024]{1,0:T(8,128)(2,1)S(1)}, bf16[128,1024]{1,0:T(8,128)(2,1)}, u32[]{:S(2)}) copy-start(bf16[128,1024]{1,0:T(8,128)(2,1)} %get-tuple-element.8) | copy-start | bytes 786436
